TPU v7x, 32 devices: a whole 2x2x4 slice. The times are simulated.
32 devices in a mesh: groups: 2 (over x), seq: 16 (over z, y, core).
Axes of the slice: x: 2, y: 2, z: 4, core: 2. Of those that a mesh axis runs over, the one named last changes fastest.
Arguments:
- tokens: bfloat16 [16384, 3584], P(('groups', 'seq')), parts along dimension 0, may hold values from -600 to 600
- token_request: int32 [16384, 1], P(('groups', 'seq')), parts along dimension 0, may hold values from 0 to 63; in each aligned block of 512 rows (0 to 511, 512 to 1023, ...) at most 32 rows name the same one
- request_slot: int32 [128], P('groups'), parts along dimension 0, may hold values from 0 to 63, each once
- new_rows: bfloat16 [128, 3584], P(('groups', 'seq')), parts along dimension 0, may hold values from -600 to 600
- queries: bfloat16 [128, 3584], P(('groups', 'seq')), parts along dimension 0, may hold values from -120 to 120
- key_cache: bfloat16 [128, 4, 128, 128], P(('groups', 'seq')), parts along dimension 0, may hold values from -6 to 6
- value_cache: bfloat16 [128, 4, 128, 128], P(('groups', 'seq')), parts along dimension 0, may hold values from -6 to 6
- cache_length: int32 [128], P(('groups', 'seq')), parts along dimension 0, may hold values from 2 to 128
- norm_gain: float32 [3584], replicated, may hold values from 0.1 to 1.9
- key_weight: bfloat16 [3584, 512], replicated, may hold values from -0.09375 to 0.09375
- value_weight: bfloat16 [3584, 512], replicated, may hold values from -0.09375 to 0.09375
- key_bias: float32 [512], replicated, may hold values from -3 to 3
- value_bias: float32 [512], replicated, may hold values from -2 to 2
- out_weight: bfloat16 [3584, 3584], P(None, 'seq'), may hold values from -0.09375 to 0.09375
Outputs:
- decoded: bfloat16 [128, 3584], P('groups', 'seq'), parts along dimension 0
There are 2 independent parts, one for each index of `groups`. A program takes and returns all parts, laid end to end along the dimension named above; an argument that names none is the same for every part. Nothing has to cross between parts.
Inputs may be any that keep to these rules, and one draw needn't show every extreme that they name: `token_request`: of the 512 tokens of one device, at most 32 belong to one request. `request_slot`: A permutation of the 64 slots.
All inputs are finite; a program needn't handle non-finite values.
Results may differ from a plain program's by a relative error of at most 0.013.
Values may be sent and summed in bfloat16 or wider, within the bound.
A program may use at most 64 MiB of HBM per device.

v0:
```python
import jax
import jax.numpy as jnp
from jax import lax
from jax.sharding import PartitionSpec as P


def project(row_data, norm_gain, key_weight, value_weight, key_bias, value_bias):
    widened = row_data.astype(jnp.float32)
    power = jnp.mean(widened * widened, axis=-1, keepdims=True)
    normed = (widened * lax.rsqrt(power + 1e-06) * norm_gain).astype(jnp.bfloat16)
    new_keys = (jnp.dot(normed, key_weight, preferred_element_type=jnp.float32) + key_bias).astype(
        jnp.bfloat16
    )
    new_values = (
        jnp.dot(normed, value_weight, preferred_element_type=jnp.float32) + value_bias
    ).astype(jnp.bfloat16)
    return (new_keys, new_values)


def rounded_back(weights):
    return lax.optimization_barrier(weights.astype(jnp.bfloat16)).astype(jnp.float32)


def cache_part(queries, key_cache, cache_length, own_keys, score_scale):
    rows_here, kv_heads, cache_size, head_dim = key_cache.shape
    grouped = queries.reshape(rows_here, kv_heads, -1, head_dim)
    cache_scores = (
        jnp.einsum("rgjd,rgcd->rgjc", grouped, key_cache, preferred_element_type=jnp.float32)
        * score_scale
    )
    visible = (
        lax.broadcasted_iota(jnp.int32, (1, 1, 1, cache_size), 3)
        < cache_length[:, None, None, None]
    )
    cache_scores = jnp.where(visible, cache_scores, -jnp.inf)
    own_scores = (
        jnp.einsum(
            "rgjd,rgd->rgj",
            grouped,
            own_keys.reshape(rows_here, kv_heads, head_dim),
            preferred_element_type=jnp.float32,
        )
        * score_scale
    )
    return (grouped, cache_scores, own_scores)


def cache_terms(cache_scores, own_scores, row_top, value_cache, own_values):
    rows_here, kv_heads, cache_size, head_dim = value_cache.shape
    cache_weights = jnp.exp(cache_scores - row_top[..., None])
    own_weights = jnp.exp(own_scores - row_top)
    totals = jnp.sum(cache_weights, axis=-1) + own_weights
    weighted_sum = jnp.einsum(
        "rgjc,rgcd->rgjd",
        cache_weights.astype(jnp.bfloat16),
        value_cache,
        preferred_element_type=jnp.float32,
    )
    weighted_sum = weighted_sum + rounded_back(own_weights)[..., None] * own_values.astype(
        jnp.float32
    ).reshape(rows_here, kv_heads, 1, head_dim)
    return (totals, weighted_sum)


def body(
    tokens,
    token_request,
    request_slot,
    new_rows,
    queries,
    key_cache,
    value_cache,
    cache_length,
    norm_gain,
    key_weight,
    value_weight,
    key_bias,
    value_bias,
    out_weight,
):
    seq_count = lax.axis_size("seq")
    rows_here, kv_heads, cache_size, head_dim = key_cache.shape
    slot_count = request_slot.shape[0]
    tok_dev = tokens.shape[0]
    heads_width = queries.shape[1]
    kv_width = kv_heads * head_dim
    capacity = max(2, 4 * tok_dev // slot_count)
    score_scale = head_dim ** (-0.5)
    fresh_keys, fresh_values = project(
        tokens, norm_gain, key_weight, value_weight, key_bias, value_bias
    )
    own_keys, own_values = project(
        new_rows, norm_gain, key_weight, value_weight, key_bias, value_bias
    )
    matches = token_request[:, 0][:, None] == lax.broadcasted_iota(jnp.int32, (1, slot_count), 1)
    token_slot = jnp.sum(jnp.where(matches, request_slot[None, :], 0), axis=1)
    grouped, cache_scores, own_scores = cache_part(
        queries, key_cache, cache_length, own_keys, score_scale
    )
    owners = token_slot // rows_here
    local_row = token_slot % rows_here
    same_slot = token_slot[:, None] == token_slot[None, :]
    earlier = lax.broadcasted_iota(jnp.int32, (tok_dev, tok_dev), 1) < lax.broadcasted_iota(
        jnp.int32, (tok_dev, tok_dev), 0
    )
    ranking = jnp.sum((same_slot & earlier).astype(jnp.int32), axis=1)
    position = (local_row * seq_count + owners) * capacity + ranking
    slot_total = rows_here * seq_count * capacity
    send_keys = jnp.zeros((slot_total, kv_width), jnp.bfloat16).at[position].set(fresh_keys)
    send_values = jnp.zeros((slot_total, kv_width), jnp.bfloat16).at[position].set(fresh_values)
    filled = jnp.zeros((slot_total,), jnp.int32).at[position].set(1)
    send_keys = send_keys.reshape(rows_here, seq_count, capacity, kv_width)
    send_values = send_values.reshape(rows_here, seq_count, capacity, kv_width)
    filled = filled.reshape(rows_here, seq_count, capacity)
    arrived_keys, arrived_values, arrived_filled = (
        lax.all_to_all(send_keys, "seq", split_axis=1, concat_axis=1, tiled=True),
        lax.all_to_all(send_values, "seq", split_axis=1, concat_axis=1, tiled=True),
        lax.all_to_all(filled, "seq", split_axis=1, concat_axis=1, tiled=True),
    )
    arrived_keys = arrived_keys.reshape(rows_here, seq_count * capacity, kv_heads, head_dim)
    arrived_values = arrived_values.reshape(rows_here, seq_count * capacity, kv_heads, head_dim)
    present = arrived_filled.reshape(rows_here, seq_count * capacity) > 0
    fresh_scores = (
        jnp.einsum("rgjd,rfgd->rgjf", grouped, arrived_keys, preferred_element_type=jnp.float32)
        * score_scale
    )
    fresh_scores = jnp.where(present[:, None, None, :], fresh_scores, -jnp.inf)
    row_top = jnp.maximum(
        jnp.maximum(jnp.max(cache_scores, axis=-1), own_scores), jnp.max(fresh_scores, axis=-1)
    )
    totals, weighted_sum = cache_terms(cache_scores, own_scores, row_top, value_cache, own_values)
    fresh_weights = jnp.exp(fresh_scores - row_top[..., None])
    totals = totals + jnp.sum(fresh_weights, axis=-1)
    weighted_sum = weighted_sum + jnp.einsum(
        "rgjf,rfgd->rgjd",
        fresh_weights.astype(jnp.bfloat16),
        arrived_values,
        preferred_element_type=jnp.float32,
    )
    head_outputs = (
        (weighted_sum / totals[..., None]).astype(jnp.bfloat16).reshape(rows_here, heads_width)
    )
    decoded = jnp.dot(
        lax.all_gather(head_outputs, "seq", axis=0, tiled=True),
        out_weight,
        preferred_element_type=jnp.float32,
    )
    return decoded.astype(jnp.bfloat16)


def solution(mesh):
    in_specs = (
        P(("groups", "seq"), None),
        P(("groups", "seq"), None),
        P("groups"),
        P(("groups", "seq"), None),
        P(("groups", "seq"), None),
        P(("groups", "seq"), None, None, None),
        P(("groups", "seq"), None, None, None),
        P(("groups", "seq")),
        P(),
        P(),
        P(),
        P(),
        P(),
        P(None, "seq"),
    )
    out_specs = P("groups", "seq")
    return jax.shard_map(body, mesh=mesh, in_specs=in_specs, out_specs=out_specs, check_vma=False)
```

profile of v0, /device:TPU:1, one launch (start us, length us, event | category | flops | bytes accessed | tf_op | source)
XLA Modules:
  0.0 165.2 jit_solution(8116839079037232777)
XLA Ops:
  0.0 0.0 copy-start
  0.0 0.0 copy-start.4
  0.0 0.0 copy-start.6
  0.0 0.9 select_reduce_fusion
  0.9 0.3 convert_reduce_fusion
  1.2 2.5 %scatter_custom_fusion = s32[2048]{0:T(1024)S(1)} fusion(s32[512]{0:T(512)S(1)} %bitcast.38, s32[512]{0:T(512)S(1)} %broadcast.180, s32[]{:T(128)} %constant.25.clone.1), kind=kCustom, calls=%fused_computation.63 | custom fusion | bytes 8196 | tf_op jit(solution)/shard_map/scatter | solution.py:111
  3.7 0.1 reshape.175
  3.8 0.7 reshape.219
  4.5 7.3 %all-to-all-start = ((s32[16,1,128]{2,1,0:T(1,128)}), s32[16,1,128]{2,1,0:T(1,128)S(1)}, u32[]{:S(2)}, u32[]{:S(2)}) async-start(s32[16,1,128]{2,1,0:T(1,128)} %reshape.219), calls=%async_computation | async-start | bytes 16384 | tf_op jit(solution)/shard_map/all_to_all | solution.py:118
  11.8 0.0 copy-start.1
  11.8 3.0 %fusion = f32[512]{0:T(512)S(1)} fusion(bf16[512,3584]{1,0:T(8,128)(2,1)} %param.14), kind=kLoop, calls=%fused_computation.5 | loop fusion | flops 5504512 | bytes 3672064 | tf_op jit(solution)/shard_map/reduce_sum | solution.py:9
  14.8 0.0 copy-done.4
  14.8 0.0 copy-done.6
  14.8 0.1 copy-done.1
  15.0 4.2 %fusion.7 = bf16[512,512]{1,0:T(8,128)(2,1)S(1)} fusion(bf16[3584,512]{1,0:T(8,128)(2,1)S(1)} %copy-done.1, bf16[512,3584]{1,0:T(8,128)(2,1)} %param.14, f32[3584]{0:T(1024)S(1)} %copy-done.4, f32[512]{0:T(512)S(1)} %add_rsqrt_fusion, f32[512]{0:T(512)S(1)} %copy-done.6), kind=kOutput, calls=%fused_computation.14 | convolution fusion | flops 1886912512 | bytes 7882752 | tf_op jit(solution)/shard_map/dot_general | solution.py:11
  19.2 4.1 %scatter_custom_fusion.1 = bf16[2048,512]{1,0:T(8,128)(2,1)} fusion(s32[512]{0:T(512)S(1)} %bitcast.39, bf16[512,512]{1,0:T(8,128)(2,1)S(1)} %fusion.7, bf16[]{:T(256)} %constant.56.clone.1), kind=kCustom, calls=%fused_computation.33 | custom fusion | bytes 2097154 | tf_op jit(solution)/shard_map/scatter | solution.py:109
  23.3 0.0 copy-start.7
  23.3 3.1 %copy.39 = bf16[4,16,32,512]{3,2,0,1:T(8,128)(2,1)} copy(bf16[4,16,32,512]{3,2,1,0:T(8,128)(2,1)} %bitcast.31) | data formatting | bytes 4194304 | tf_op jit(solution)/shard_map/reshape | solution.py:112
  26.4 0.0 all-to-all-done
  26.4 6.0 %all-to-all-start.1 = ((bf16[4,16,32,512]{3,2,0,1:T(8,128)(2,1)}), bf16[4,16,32,512]{3,2,0,1:T(8,128)(2,1)}, u32[]{:S(2)}, u32[]{:S(2)}) async-start(bf16[4,16,32,512]{3,2,0,1:T(8,128)(2,1)} %copy.39), calls=%async_computation.1 | async-start | bytes 4194304 | tf_op jit(solution)/shard_map/all_to_all | solution.py:116
  32.4 0.0 copy-done.7
  32.4 5.3 %fusion.8 = bf16[512,512]{1,0:T(8,128)(2,1)S(1)} fusion(bf16[3584,512]{1,0:T(8,128)(2,1)} %param.24, bf16[512,3584]{1,0:T(8,128)(2,1)} %param.14, f32[3584]{0:T(1024)S(1)} %copy-done.4, f32[512]{0:T(512)S(1)} %add_rsqrt_fusion, f32[512]{0:T(512)S(1)} %copy-done.7), kind=kOutput, calls=%fused_computation.15 | convolution fusion | flops 1886912512 | bytes 7882752 | tf_op jit(solution)/shard_map/dot_general | solution.py:15
  37.7 4.1 %scatter_custom_fusion.2 = bf16[2048,512]{1,0:T(8,128)(2,1)} fusion(s32[512]{0:T(512)S(1)} %bitcast.40, bf16[512,512]{1,0:T(8,128)(2,1)S(1)} %fusion.8, bf16[]{:T(256)} %constant.56.clone.1), kind=kCustom, calls=%fused_computation.31 | custom fusion | bytes 2097154 | tf_op jit(solution)/shard_map/scatter | solution.py:110
  41.8 0.0 copy-start.5
  41.8 0.0 copy-start.3
  41.8 3.2 %copy.42 = bf16[4,16,32,512]{3,2,0,1:T(8,128)(2,1)} copy(bf16[4,16,32,512]{3,2,1,0:T(8,128)(2,1)} %bitcast.30) | data formatting | bytes 4194304 | tf_op jit(solution)/shard_map/reshape | solution.py:113
  45.0 29.0 %all-to-all-done.1 = bf16[4,16,32,512]{3,2,0,1:T(8,128)(2,1)} async-done(((bf16[4,16,32,512]{3,2,0,1:T(8,128)(2,1)}), bf16[4,16,32,512]{3,2,0,1:T(8,128)(2,1)}, u32[]{:S(2)}, u32[]{:S(2)}) %all-to-all-start.1) | async-done | bytes 2097184 | tf_op jit(solution)/shard_map/all_to_all | solution.py:116
  74.0 10.9 %all-to-all-start.2 = ((bf16[4,16,32,512]{3,2,0,1:T(8,128)(2,1)}), bf16[4,16,32,512]{3,2,0,1:T(8,128)(2,1)}, u32[]{:S(2)}, u32[]{:S(2)}) async-start(bf16[4,16,32,512]{3,2,0,1:T(8,128)(2,1)} %copy.42), calls=%async_computation.2 | async-start | bytes 4194304 | tf_op jit(solution)/shard_map/all_to_all | solution.py:117
  84.9 0.0 copy-done.5
  84.9 0.0 copy-done.3
  84.9 0.1 fusion.44
  85.1 0.0 copy-start.9
  85.1 0.0 copy-start.2
  85.1 2.7 %fusion.28 = bf16[4,512]{1,0:T(4,128)(2,1)S(1)} fusion(bf16[3584,512]{1,0:T(8,128)(2,1)} %param.23, f32[512]{0:T(512)S(1)} %copy-done.6, bf16[4,3584]{1,0:T(4,128)(2,1)S(1)} %copy-done.3, f32[3584]{0:T(1024)S(1)} %copy-done.4, f32[4]{0:T(128)S(1)} %add_rsqrt_fusion.1), kind=kOutput, calls=%fused_computation.28 | convolution fusion | flops 14741504 | bytes 3719184 | tf_op jit(solution)/shard_map/dot_general | solution.py:11
  87.8 2.7 %fusion.30 = f32[4,512]{1,0:T(4,128)S(1)} fusion(bf16[3584,512]{1,0:T(8,128)(2,1)} %param.24, f32[512]{0:T(512)S(1)} %copy-done.7, bf16[4,3584]{1,0:T(4,128)(2,1)S(1)} %copy-done.3, f32[3584]{0:T(1024)S(1)} %copy-done.4, f32[4]{0:T(128)S(1)} %add_rsqrt_fusion.1), kind=kOutput, calls=%fused_computation.30 | convolution fusion | flops 14743552 | bytes 3723280 | tf_op jit(solution)/shard_map/dot_general | solution.py:15
  90.5 0.0 copy-done.9
  90.5 0.1 iota_compare_fusion.2
  90.6 0.1 fusion.58
  90.7 0.0 copy-done.2
  90.7 0.5 fusion.57
  91.2 0.5 broadcast.190
  91.7 0.7 reduce
  92.4 0.1 reshape.220
  92.5 0.1 gt.15
  92.6 3.2 %copy.40 = bf16[4,16,32,512]{3,2,1,0:T(8,128)(2,1)} copy(bf16[4,16,32,512]{3,2,0,1:T(8,128)(2,1)} %all-to-all-done.1) | data formatting | bytes 4194304 | tf_op jit(solution)/shard_map/all_to_all | solution.py:116
  95.8 4.0 %reshape.177 = bf16[4,512,4,128]{3,2,1,0:T(4,128)(2,1)} reshape(bf16[4,16,32,512]{3,2,1,0:T(8,128)(2,1)} %copy.40) | data formatting | bytes 4194304 | tf_op jit(solution)/shard_map/reshape | solution.py:120
  99.7 2.3 %fusion.56 = (f32[4,4,7]{2,1,0:T(4,128)S(1)}, f32[4,4,7,512]{3,2,1,0:T(8,128)S(1)}) fusion(bf16[4,4,7,128]{3,2,1,0:T(8,128)(2,1)S(1)} %reshape.173, bf16[4,512,4,128]{3,2,1,0:T(4,128)(2,1)} %reshape.177, pred[4,512]{1,0:T(4,128)(4,1)S(1)} %gt.15), kind=kOutput, calls=%fused_computation.71 | convolution fusion | flops 14851984 | bytes 2357696 | tf_op jit(solution)/shard_map/rgjd,rfgd->rgjf/dot_general | solution.py:124
  102.1 0.2 fusion.42
  102.3 0.2 fusion.38
  102.5 0.0 copy-start.8
  102.5 23.9 %all-to-all-done.2 = bf16[4,16,32,512]{3,2,0,1:T(8,128)(2,1)} async-done(((bf16[4,16,32,512]{3,2,0,1:T(8,128)(2,1)}), bf16[4,16,32,512]{3,2,0,1:T(8,128)(2,1)}, u32[]{:S(2)}, u32[]{:S(2)}) %all-to-all-start.2) | async-done | bytes 2097184 | tf_op jit(solution)/shard_map/all_to_all | solution.py:117
  126.4 3.2 %copy.43 = bf16[4,16,32,512]{3,2,1,0:T(8,128)(2,1)} copy(bf16[4,16,32,512]{3,2,0,1:T(8,128)(2,1)} %all-to-all-done.2) | data formatting | bytes 4194304 | tf_op jit(solution)/shard_map/all_to_all | solution.py:117
  129.6 4.0 %reshape.179 = bf16[4,512,4,128]{3,2,1,0:T(4,128)(2,1)} reshape(bf16[4,16,32,512]{3,2,1,0:T(8,128)(2,1)} %copy.43) | data formatting | bytes 4194304 | tf_op jit(solution)/shard_map/reshape | solution.py:121
  133.6 0.0 copy-done.8
  133.6 0.3 convolution_add_fusion.2
  133.9 2.0 %fusion.25 = bf16[4,4,7,128]{3,2,1,0:T(8,128)(2,1)S(1)} fusion(f32[4,4,7,128]{3,2,1,0:T(8,128)S(1)} %convolution_add_fusion.2, bf16[4,512,4,128]{3,2,1,0:T(4,128)(2,1)} %reshape.179, f32[4,4,7,512]{3,2,1,0:T(8,128)S(1)} %get-tuple-element.8, f32[4,4,7]{2,1,0:T(4,128)S(1)} %get-tuple-element.6, f32[4,4,7]{2,1,0:T(4,128)S(1)} %add_add_fusion), kind=kOutput, calls=%fused_computation.25 | convolution fusion | flops 14837760 | bytes 2413440 | tf_op jit(solution)/shard_map/rgjf,rfgd->rgjd/dot_general | solution.py:134
  136.0 27.8 %all-gather = bf16[16,4,3584]{2,1,0:T(4,128)(2,1)S(1)} all-gather(bf16[1,4,3584]{2,1,0:T(4,128)(2,1)S(1)} %reshape.206), channel_id=1, replica_groups=mesh['groups'=2,'seq'=16] {'seq'}, dimensions={0}, use_global_device_ids=true | all-gather | bytes 487424 | tf_op jit(solution)/shard_map/all_gather | solution.py:144
  163.8 0.1 reshape.207
  163.9 0.0 copy-done
  164.0 1.2 convolution_convert_fusion
  (13 shorter events, 0.2 us)
Async XLA Ops:
  0.0 163.9 %copy-start = (bf16[3584,224]{0,1:T(8,128)(2,1)S(1)}, bf16[3584,224]{0,1:T(8,128)(2,1)}, u32[]{:S(2)}) copy-start(bf16[3584,224]{0,1:T(8,128)(2,1)} %param.27) | copy-start | bytes 4816900
  0.0 14.8 %copy-start.4 = (f32[3584]{0:T(1024)S(1)}, f32[3584]{0:T(1024)}, u32[]{:S(2)}) copy-start(f32[3584]{0:T(1024)} %param.22) | copy-start | bytes 43012
  0.0 14.8 %copy-start.6 = (f32[512]{0:T(512)S(1)}, f32[512]{0:T(512)}, u32[]{:S(2)}) copy-start(f32[512]{0:T(512)} %param.25) | copy-start | bytes 6148
  4.5 21.9 %all-to-all-start = ((s32[16,1,128]{2,1,0:T(1,128)}), s32[16,1,128]{2,1,0:T(1,128)S(1)}, u32[]{:S(2)}, u32[]{:S(2)}) async-start(s32[16,1,128]{2,1,0:T(1,128)} %reshape.219), calls=%async_computation | async-start | bytes 16384 | tf_op jit(solution)/shard_map/all_to_all | solution.py:118
  11.8 3.1 %copy-start.1 = (bf16[3584,512]{1,0:T(8,128)(2,1)S(1)}, bf16[3584,512]{1,0:T(8,128)(2,1)}, u32[]{:S(2)}) copy-start(bf16[3584,512]{1,0:T(8,128)(2,1)} %param.23) | copy-start | bytes 11010052
  23.3 9.2 %copy-start.7 = (f32[512]{0:T(512)S(1)}, f32[512]{0:T(512)}, u32[]{:S(2)}) copy-start(f32[512]{0:T(512)} %param.26) | copy-start | bytes 6148
  26.4 47.6 %all-to-all-start.1 = ((bf16[4,16,32,512]{3,2,0,1:T(8,128)(2,1)}), bf16[4,16,32,512]{3,2,0,1:T(8,128)(2,1)}, u32[]{:S(2)}, u32[]{:S(2)}) async-start(bf16[4,16,32,512]{3,2,0,1:T(8,128)(2,1)} %copy.39), calls=%async_computation.1 | async-start | bytes 4194304 | tf_op jit(solution)/shard_map/all_to_all | solution.py:116
  41.8 43.1 %copy-start.5 = (bf16[4,3584]{1,0:T(4,128)(2,1)S(1)}, bf16[4,3584]{1,0:T(4,128)(2,1)}, u32[]{:S(2)}) copy-start(bf16[4,3584]{1,0:T(4,128)(2,1)} %param.18) | copy-start | bytes 86020
  41.8 43.1 %copy-start.3 = (bf16[4,3584]{1,0:T(4,128)(2,1)S(1)}, bf16[4,3584]{1,0:T(4,128)(2,1)}, u32[]{:S(2)}) copy-start(bf16[4,3584]{1,0:T(4,128)(2,1)} %param.17) | copy-start | bytes 86020
  74.0 52.4 %all-to-all-start.2 = ((bf16[4,16,32,512]{3,2,0,1:T(8,128)(2,1)}), bf16[4,16,32,512]{3,2,0,1:T(8,128)(2,1)}, u32[]{:S(2)}, u32[]{:S(2)}) async-start(bf16[4,16,32,512]{3,2,0,1:T(8,128)(2,1)} %copy.42), calls=%async_computation.2 | async-start | bytes 4194304 | tf_op jit(solution)/shard_map/all_to_all | solution.py:117
  85.1 5.4 %copy-start.9 = (s32[4]{0:T(128)S(1)}, s32[4]{0:T(128)}, u32[]{:S(2)}) copy-start(s32[4]{0:T(128)} %param.21) | copy-start | bytes 52
  85.1 5.6 %copy-start.2 = (bf16[4,4,128,128]{3,2,1,0:T(8,128)(2,1)S(1)}, bf16[4,4,128,128]{3,2,1,0:T(8,128)(2,1)}, u32[]{:S(2)}) copy-start(bf16[4,4,128,128]{3,2,1,0:T(8,128)(2,1)} %param.19) | copy-start | bytes 1572868
  102.5 31.1 %copy-start.8 = (bf16[4,4,128,128]{3,2,1,0:T(8,128)(2,1)S(1)}, bf16[4,4,128,128]{3,2,1,0:T(8,128)(2,1)}, u32[]{:S(2)}) copy-start(bf16[4,4,128,128]{3,2,1,0:T(8,128)(2,1)} %param.20) | copy-start | bytes 1572868
where the time goes:
time: 166 us; the launch traced here: 165 us
  waiting for transfers between devices  52.9 us (32%)
  local copies, waits for them, and re-layouts  33.1 us (20%)
  blocking collectives  27.8 us (17%)
  starting transfers between devices  24.2 us (15%)
  matrix products  21.3 us (13%)
  other arithmetic  5.51 us (3%)
    all_to_all x1, waiting for transfers between devices, body(): lax.all_to_all(send_keys, 'seq', split_axis=1, concat_axis=1, tiled=True)  29 us
    all_gather x1, blocking collectives, body(): lax.all_gather(head_outputs, 'seq', axis=0, tiled=True)  27.8 us
    all_to_all x1, waiting for transfers between devices, body(): lax.all_to_all(send_values, 'seq', split_axis=1, concat_axis=1, tiled=True)  23.9 us
    all_to_all x1, starting transfers between devices, body(): lax.all_to_all(send_values, 'seq', split_axis=1, concat_axis=1, tiled=True)  10.9 us
    dot_general x2, matrix products, project(): jnp.dot(normed, value_weight, preferred_element_type=jnp.float32)  7.93 us
    all_to_all x1, starting transfers between devices, body(): lax.all_to_all(filled, 'seq', split_axis=1, concat_axis=1, tiled=True)  7.35 us
    dot_general x2, matrix products, project(): jnp.dot(normed, key_weight, preferred_element_type=jnp.float32) + key_bias  6.92 us
    all_to_all x1, starting transfers between devices, body(): lax.all_to_all(send_keys, 'seq', split_axis=1, concat_axis=1, tiled=True)  6.03 us
  transfers between devices with their start and end apart: 3, of which 2 were waited for; matrix products, arithmetic and copies ran while one was open for 27% of the time, Pallas kernels for 0%

commit v1 on v0

v1 whole, which is shorter than its diff:
```python
import functools

import jax
import jax.numpy as jnp
from jax import lax
from jax.experimental import pallas as pl
from jax.experimental.pallas import tpu as pltpu
from jax.sharding import PartitionSpec as P

MESH = pl.DeviceIdType.MESH
NT = (((1,), (1,)), ((), ()))
LOW = -1e30


def kernel(
    dims,
    token_request,
    request_slot,
    new_rows,
    queries,
    cache_length,
    norm_gain,
    key_bias,
    value_bias,
    tokens_hbm,
    key_weight_hbm,
    value_weight_hbm,
    out_weight_hbm,
    key_cache_hbm,
    value_cache_hbm,
    out,
    tok,
    kw,
    vw,
    ow,
    kc,
    vc,
    xn,
    qstage,
    qall,
    slots,
    kvl,
    kvr,
    part,
    rpart,
    stat,
    rstat,
    hstage,
    hall,
    load_sem,
    qs_sem,
    qr_sem,
    sib_s,
    sib_r,
    ps_sem,
    pr_sem,
    ss_sem,
    sr_sem,
    hs_sem,
    hr_sem,
    fs_sem,
    fr_sem,
):
    nk, rows_here, kv_heads, group, head_dim = dims
    f32, bf16 = jnp.float32, jnp.bfloat16
    tok_dev, width = tok.shape
    block = qall.shape[2]
    chunks = 4
    chunk = tok_dev // chunks
    me = lax.axis_index("seq")
    mek, mec = me // 2, me % 2
    sibling = mek * 2 + (1 - mec)

    def ahead(i):
        return lax.rem(mek + i, nk)

    def behind(i):
        return lax.rem(mek + nk - i, nk)

    def peer(k):
        return {"seq": k * 2 + mec}

    loads = []

    def load(src, dst):
        c = pltpu.make_async_copy(src, dst, load_sem.at[len(loads)])
        c.start()
        loads.append(c)
        return c

    tok_loads = [
        load(tokens_hbm.at[pl.ds(c * chunk, chunk)], tok.at[pl.ds(c * chunk, chunk)])
        for c in range(chunks)
    ]
    kw_load = load(key_weight_hbm, kw)
    vw_load = load(value_weight_hbm, vw)
    kc_load = load(key_cache_hbm, kc)
    vc_load = load(value_cache_hbm, vc)
    ow_load = load(out_weight_hbm, ow)

    barrier = pltpu.get_barrier_semaphore()
    pl.semaphore_signal(barrier, inc=1, device_id={"seq": sibling}, device_id_type=MESH)
    for i in range(1, nk):
        pl.semaphore_signal(barrier, inc=1, device_id=peer(ahead(i)), device_id_type=MESH)

    qstage[...] = jnp.zeros_like(qstage)
    q_wide = queries[...].astype(f32)
    for g in range(kv_heads):
        for j in range(group):
            h = g * group + j
            qstage[g, j * rows_here : (j + 1) * rows_here, :] = q_wide[
                :, h * head_dim : (h + 1) * head_dim
            ]
    for g in range(kv_heads):
        qall[0, g] = qstage[g].astype(bf16)

    slot_total = request_slot.shape[0]
    matches = token_request[...] == lax.broadcasted_iota(jnp.int32, (slot_total, tok_dev), 0)
    slot_row = jnp.sum(
        jnp.where(matches, request_slot[...].astype(f32), 0.0), axis=0, keepdims=True
    ).astype(jnp.int32)
    slots[0] = jnp.broadcast_to(slot_row, (8, tok_dev))

    pl.semaphore_wait(barrier, nk)

    def remote(src, dst, s, r, device):
        c = pltpu.make_async_remote_copy(
            src_ref=src, dst_ref=dst, send_sem=s, recv_sem=r, device_id=device, device_id_type=MESH
        )
        c.start()
        return c

    started = []
    q_copies = {}
    for i in range(1, nk):
        q_copies[i] = remote(qall.at[0], qall.at[i], qs_sem.at[i], qr_sem.at[i], peer(ahead(i)))
    slot_copy = remote(slots.at[0], slots.at[1], sib_s.at[2], sib_r.at[2], {"seq": sibling})

    gain = norm_gain[...]

    def normed(x):
        power = jnp.mean(x * x, axis=-1, keepdims=True)
        return (x * lax.rsqrt(power + 1e-06) * gain).astype(bf16)

    fresh = jnp.concatenate(
        [new_rows[...].astype(f32), jnp.zeros((16 - rows_here, width), f32)], axis=0
    )
    xn[tok_dev : tok_dev + 16, :] = normed(fresh)
    for c in range(chunks):
        tok_loads[c].wait()

        @pl.loop(c * chunk // 16, (c + 1) * chunk // 16)
        def _(b):
            at = pl.ds(pl.multiple_of(b * 16, 16), 16)
            xn[at, :] = normed(tok[at, :].astype(f32))

    kv_copies = []
    half = kw.shape[1] // 2
    for hf in range(2):
        cols = slice(hf * half, (hf + 1) * half)
        for n, (w, b, w_load) in enumerate(((kw, key_bias, kw_load), (vw, value_bias, vw_load))):
            if hf == 0:
                w_load.wait()
            kvl[hf, :, n * half : (n + 1) * half] = (
                jnp.dot(xn[...], w[:, cols], preferred_element_type=f32) + b[:, cols]
            ).astype(bf16)
        kv_copies.append(
            remote(
                kvl.at[hf, pl.ds(0, tok_dev)],
                kvr.at[hf],
                sib_s.at[hf],
                sib_r.at[hf],
                {"seq": sibling},
            )
        )

    for i in range(1, nk):
        q_copies[i].wait_recv()
    slot_copy.wait_recv()

    scale = head_dim ** (-0.5)
    per_half = kv_heads // 2
    per_chunk = min(4, nk)
    chunk_rows = per_chunk * block
    p_copies = {}
    for hf in range(2):
        kv_copies[hf].wait_recv()
        for q0 in range(0, nk, per_chunk):
            lane = lax.broadcasted_iota(jnp.int32, (block, 128), 0) % rows_here
            row_slot = jnp.concatenate(
                [(behind(q0 + i) * 2 + mec) * rows_here + lane for i in range(per_chunk)], axis=0
            )[:, :1]
            mask_l = row_slot == slots[0, 0:1, :]
            mask_r = row_slot == slots[1, 0:1, :]
            lses = []
            for gl in range(per_half):
                g = hf * per_half + gl
                q = qall[q0 : q0 + per_chunk, g].reshape(chunk_rows, head_dim)
                kcols = slice(gl * head_dim, (gl + 1) * head_dim)
                vcols = slice(half + gl * head_dim, half + (gl + 1) * head_dim)
                s_l = lax.dot_general(q, kvl[hf, :tok_dev, kcols], NT, preferred_element_type=f32)
                s_r = lax.dot_general(q, kvr[hf, :, kcols], NT, preferred_element_type=f32)
                s_l = jnp.where(mask_l, s_l * scale, LOW)
                s_r = jnp.where(mask_r, s_r * scale, LOW)
                top = jnp.max(jnp.maximum(s_l, s_r), axis=-1, keepdims=True)
                p_l = jnp.exp(s_l - top)
                p_r = jnp.exp(s_r - top)
                total = jnp.sum(p_l + p_r, axis=-1, keepdims=True)
                o = jnp.dot(
                    p_l.astype(bf16), kvl[hf, :tok_dev, vcols], preferred_element_type=f32
                ) + jnp.dot(p_r.astype(bf16), kvr[hf, :, vcols], preferred_element_type=f32)
                o = (o / total).astype(bf16)
                part[hf, q0 : q0 + per_chunk, gl] = o.reshape(per_chunk, block, head_dim)
                lses.append(top + jnp.log(total))
            which = lax.broadcasted_iota(jnp.int32, (chunk_rows, 128), 1)
            packed = jnp.where(which == 0, lses[0], jnp.where(which == 1, lses[1], 0.0))
            stat[hf, q0 // per_chunk] = packed.T[:8, :]
            for i in range(q0, q0 + per_chunk):
                if i > 0:
                    p_copies[hf, i] = (
                        remote(
                            part.at[hf, i],
                            rpart.at[hf, i],
                            ps_sem.at[hf, i],
                            pr_sem.at[hf, i],
                            peer(behind(i)),
                        ),
                        remote(
                            stat.at[hf, i // per_chunk],
                            rstat.at[hf, i],
                            ss_sem.at[hf, i],
                            sr_sem.at[hf, i],
                            peer(behind(i)),
                        ),
                    )

    kc_load.wait()
    vc_load.wait()
    row_of = lax.broadcasted_iota(jnp.int32, (block, 128), 0) % rows_here
    place = lax.broadcasted_iota(jnp.int32, (block, 128), 1)
    visible = [(row_of == r) & (place < cache_length[r]) for r in range(rows_here)]
    own = []
    for g in range(kv_heads):
        hf, gl = g // per_half, g % per_half
        q = qall[0, g]
        s_c = jnp.full((block, 128), LOW, f32)
        for r in range(rows_here):
            s = lax.dot_general(q, kc[r, g], NT, preferred_element_type=f32) * scale
            s_c = jnp.where(visible[r], s, s_c)
        new = kvl[hf, tok_dev : tok_dev + 16, :].astype(f32)[:rows_here]
        k_new = new[:, gl * head_dim : (gl + 1) * head_dim]
        v_new = new[:, half + gl * head_dim : half + (gl + 1) * head_dim]
        k_new = jnp.concatenate([k_new] * (block // rows_here), axis=0)
        v_new = jnp.concatenate([v_new] * (block // rows_here), axis=0)
        s_o = jnp.sum(q.astype(f32) * k_new, axis=-1, keepdims=True) * scale
        top = jnp.maximum(jnp.max(s_c, axis=-1, keepdims=True), s_o)
        p_c = jnp.exp(s_c - top)
        p_o = jnp.exp(s_o - top)
        total = jnp.sum(p_c, axis=-1, keepdims=True) + p_o
        acc = p_o.astype(bf16).astype(f32) * v_new
        for r in range(rows_here):
            acc = acc + jnp.dot(
                jnp.where(row_of == r, p_c, 0.0).astype(bf16), vc[r, g], preferred_element_type=f32
            )
        own.append((top, total, acc))

    for hf in range(2):
        for i in range(1, nk):
            for c in p_copies[hf, i]:
                c.wait_recv()
        rstat[hf, 0] = stat[hf, 0]
        flat = rstat[hf].reshape(nk * 8, 128)
        pad = -(nk * 8) % 128
        if pad:
            flat = jnp.concatenate([flat, jnp.zeros((pad, 128), f32)], axis=0)
        turned = flat.T
        for gl in range(per_half):
            g = hf * per_half + gl
            top, total, acc = own[g]
            cols = []
            for i in range(nk):
                r0 = (i % per_chunk) * block
                cols.append(turned[r0 : r0 + block, i * 8 + gl : i * 8 + gl + 1])
            best = top
            for col in cols:
                best = jnp.maximum(best, col)
            w = jnp.exp(top - best)
            total = total * w
            acc = acc * w
            for i in range(nk):
                w = jnp.exp(cols[i] - best)
                total = total + w
                piece = part[hf, 0, gl] if i == 0 else rpart[hf, i, gl]
                acc = acc + w * piece.astype(f32)
            result = acc / total
            for j in range(group):
                hstage[
                    g * rows_here : (g + 1) * rows_here, j * head_dim : (j + 1) * head_dim
                ] = result[j * rows_here : (j + 1) * rows_here, :]
    hall[me] = hstage[...].astype(bf16)

    h_copies = {}
    for i in range(1, nk):
        h_copies[i] = remote(
            hall.at[me], hall.at[me], hs_sem.at[i], hr_sem.at[i], peer(ahead(i))
        )
    f_copies = {}
    f_copies[0] = remote(hall.at[me], hall.at[me], fs_sem.at[0], fr_sem.at[0], {"seq": sibling})
    for i in range(1, nk):
        h_copies[i].wait_recv()
        at = behind(i) * 2 + mec
        f_copies[i] = remote(
            hall.at[at], hall.at[at], fs_sem.at[i], fr_sem.at[i], {"seq": sibling}
        )
    ow_load.wait()
    for i in range(nk):
        f_copies[i].wait_recv()

    rows_all = hall.shape[0] * 16
    flat = hall[...].reshape(rows_all, hall.shape[2])
    slot_at = lax.broadcasted_iota(jnp.int32, (slot_total, rows_all), 0)
    row_at = lax.broadcasted_iota(jnp.int32, (slot_total, rows_all), 1)
    acc = None
    for g in range(kv_heads):
        want = (slot_at // rows_here) * 16 + g * rows_here + slot_at % rows_here
        pick = jnp.where(row_at == want, 1.0, 0.0).astype(bf16)
        a = jnp.dot(pick, flat, preferred_element_type=f32).astype(bf16)
        span = group * head_dim
        term = jnp.dot(a, ow[g * span : (g + 1) * span, :], preferred_element_type=f32)
        acc = term if acc is None else acc + term
    out[...] = acc.astype(bf16)

    for i in range(1, nk):
        q_copies[i].wait_send()
        h_copies[i].wait_send()
        for hf in range(2):
            for c in p_copies[hf, i]:
                c.wait_send()
    for i in range(nk):
        f_copies[i].wait_send()
    slot_copy.wait_send()
    for c in kv_copies:
        c.wait_send()


def body(
    tokens,
    token_request,
    request_slot,
    new_rows,
    queries,
    key_cache,
    value_cache,
    cache_length,
    norm_gain,
    key_weight,
    value_weight,
    key_bias,
    value_bias,
    out_weight,
):
    seq_count = lax.axis_size("seq")
    nk = seq_count // 2
    rows_here, kv_heads, cache_size, head_dim = key_cache.shape
    slot_count = request_slot.shape[0]
    tok_dev, width = tokens.shape
    group = queries.shape[1] // (kv_heads * head_dim)
    kv_width = kv_heads * head_dim
    block = 32
    f32, bf16, i32 = jnp.float32, jnp.bfloat16, jnp.int32
    vmem = pl.BlockSpec(memory_space=pltpu.VMEM)
    smem = pl.BlockSpec(memory_space=pltpu.SMEM)
    hbm = pl.BlockSpec(memory_space=pl.ANY)
    dma = pltpu.SemaphoreType.DMA
    dims = (nk, rows_here, kv_heads, group, head_dim)
    return pl.pallas_call(
        functools.partial(kernel, dims),
        out_shape=jax.ShapeDtypeStruct((slot_count, out_weight.shape[1]), bf16),
        in_specs=[vmem, vmem, vmem, vmem, smem, vmem, vmem, vmem] + [hbm] * 6,
        out_specs=vmem,
        scratch_shapes=[
            pltpu.VMEM((tok_dev, width), bf16),
            pltpu.VMEM((width, kv_width), bf16),
            pltpu.VMEM((width, kv_width), bf16),
            pltpu.VMEM(out_weight.shape, bf16),
            pltpu.VMEM(key_cache.shape, bf16),
            pltpu.VMEM(value_cache.shape, bf16),
            pltpu.VMEM((tok_dev + 16, width), bf16),
            pltpu.VMEM((kv_heads, block, head_dim), f32),
            pltpu.VMEM((nk, kv_heads, block, head_dim), bf16),
            pltpu.VMEM((2, 8, tok_dev), i32),
            pltpu.VMEM((2, tok_dev + 16, kv_width), bf16),
            pltpu.VMEM((2, tok_dev, kv_width), bf16),
            pltpu.VMEM((2, nk, kv_heads // 2, block, head_dim), bf16),
            pltpu.VMEM((2, nk, kv_heads // 2, block, head_dim), bf16),
            pltpu.VMEM((2, nk // 4, 8, 128), f32),
            pltpu.VMEM((2, nk, 8, 128), f32),
            pltpu.VMEM((16, group * head_dim), f32),
            pltpu.VMEM((seq_count, 16, group * head_dim), bf16),
            dma((9,)),
            dma((nk,)),
            dma((nk,)),
            dma((3,)),
            dma((3,)),
            dma((2, nk)),
            dma((2, nk)),
            dma((2, nk)),
            dma((2, nk)),
            dma((nk,)),
            dma((nk,)),
            dma((nk,)),
            dma((nk,)),
        ],
        compiler_params=pltpu.CompilerParams(
            collective_id=0, has_side_effects=True, vmem_limit_bytes=52 * 1024 * 1024
        ),
    )(
        token_request.reshape(1, tok_dev),
        request_slot.reshape(slot_count, 1),
        new_rows,
        queries,
        cache_length,
        norm_gain.reshape(1, width),
        key_bias.reshape(1, kv_width),
        value_bias.reshape(1, kv_width),
        tokens,
        key_weight,
        value_weight,
        out_weight,
        key_cache,
        value_cache,
    )


def solution(mesh):
    in_specs = (
        P(("groups", "seq"), None),
        P(("groups", "seq"), None),
        P("groups"),
        P(("groups", "seq"), None),
        P(("groups", "seq"), None),
        P(("groups", "seq"), None, None, None),
        P(("groups", "seq"), None, None, None),
        P(("groups", "seq")),
        P(),
        P(),
        P(),
        P(),
        P(),
        P(None, "seq"),
    )
    out_specs = P("groups", "seq")
    return jax.shard_map(body, mesh=mesh, in_specs=in_specs, out_specs=out_specs, check_vma=False)
```

time: 166 us -> 46.9 us (0.28)
  waiting for transfers between devices: 52.9 us -> 0 us
  Pallas kernels: 0 us -> 36.4 us
  blocking collectives: 27.8 us -> 0 us
  starting transfers between devices: 24.2 us -> 0 us
  local copies, waits for them, and re-layouts: 33.1 us -> 10.1 us
  matrix products: 21.3 us -> 0 us
  other arithmetic: 5.51 us -> 0 us
    all_to_all x3 -> x0, waiting for transfers between devices: 52.9 us -> none  [the longest x1 29 us: body(): lax.all_to_all(send_keys, 'seq', split_axis=1, concat_axis=1, tiled=True)]
    pallas_call x0 -> x1, Pallas kernels: none -> 36.4 us  [body(): pl.pallas_call(functools.partial(kernel, dims), out_shape=jax.ShapeDtypeS...]
    all_gather x1 -> x0, blocking collectives: 27.8 us -> none  [body(): lax.all_gather(head_outputs, 'seq', axis=0, tiled=True)]
    all_to_all x3 -> x0, starting transfers between devices: 24.2 us -> none  [the longest x1 10.9 us: body(): lax.all_to_all(send_values, 'seq', split_axis=1, concat_axis=1, tiled=True)]
    dot_general x10 -> x0, matrix products: 21.3 us -> none  [the longest x2 7.93 us: project(): jnp.dot(normed, value_weight, preferred_element_type=jnp.float32)]
    reshape x8 -> x2, local copies, waits for them, and re-layouts: 14.4 us -> 1.56 us  [the longest x1 0.82 us: body(): norm_gain.reshape(1, width)]
    scatter x3 -> x0, local copies, waits for them, and re-layouts: 10.6 us -> none  [the longest x1 4.09 us: body(): jnp.zeros((slot_total, kv_width), jnp.bfloat16).at[position].set(fresh_keys)]
    unnamed x24 -> x18, local copies, waits for them, and re-layouts: 1.08 us -> 8.52 us
  transfers between devices with their start and end apart: 3 -> 0, of which waited for: 2 -> 0; matrix products, arithmetic and copies ran while one was open for 27% -> 0% of each run, Pallas kernels for 0% -> 0%
where the time goes in v1:
time: 46.9 us; the launch traced here: 46.5 us
  Pallas kernels  36.4 us (78%)
  local copies, waits for them, and re-layouts  10.1 us (22%)
    pallas_call x1, Pallas kernels, body(): pl.pallas_call(functools.partial(kernel, dims), out_shape=jax.ShapeDtypeS...  36.4 us
    unnamed x18, local copies, waits for them, and re-layouts  8.52 us

profile of v1, /device:TPU:1, one launch (start us, length us, event | category | flops | bytes accessed | tf_op | source)
XLA Modules:
  0.0 46.5 jit_solution(17006825115639643581)
XLA Ops:
  0.0 0.0 copy-start.1
  0.0 0.0 copy-start
  0.0 0.8 %reshape.17.norm_gain = f32[1,3584]{1,0:T(1,128)S(1)} reshape(f32[3584]{0:T(1024)} %param.22) | data formatting | bytes 28672 | tf_op jit(solution)/shard_map/reshape | solution.py:423
  0.8 0.7 %copy.15.request_slot = s32[64,1]{1,0:T(8,128)S(1)} copy(s32[64,1]{0,1:T(1,128)} %bitcast.7) | data formatting | bytes 512 | tf_op jit(solution)/shard_map/reshape | solution.py:419
  1.6 3.7 %copy.16.out_weight_hbm = bf16[3584,224]{1,0:T(8,128)(2,1)} copy(bf16[3584,224]{0,1:T(8,128)(2,1)} %param.27) | data formatting | bytes 3211264 | tf_op args[13]
  5.3 0.0 copy-done.1
  5.3 0.0 copy-done
  5.3 0.0 copy-start.2
  5.3 0.7 %copy-done.2 = bf16[4,3584]{1,0:T(4,128)(2,1)S(1)} copy-done((bf16[4,3584]{1,0:T(4,128)(2,1)S(1)}, bf16[4,3584]{1,0:T(4,128)(2,1)}, u32[]{:S(2)}) %copy-start.2) | copy-done | bytes 28696
  6.0 0.0 copy-start.3
  6.0 0.7 %copy-done.3 = bf16[4,3584]{1,0:T(4,128)(2,1)S(1)} copy-done((bf16[4,3584]{1,0:T(4,128)(2,1)S(1)}, bf16[4,3584]{1,0:T(4,128)(2,1)}, u32[]{:S(2)}) %copy-start.3) | copy-done | bytes 28696
  6.8 0.0 copy-start.4
  6.8 0.7 %copy-done.4 = s32[512,1]{0,1:T(1,128)S(1)} copy-done((s32[512,1]{0,1:T(1,128)S(1)}, s32[512,1]{0,1:T(1,128)}, u32[]{:S(2)}) %copy-start.4) | copy-done | bytes 2072
  7.5 0.0 copy-start.5
  7.5 0.7 %copy-done.5 = f32[512]{0:T(512)S(1)} copy-done((f32[512]{0:T(512)S(1)}, f32[512]{0:T(512)}, u32[]{:S(2)}) %copy-start.5) | copy-done | bytes 2072
  8.1 0.0 copy-start.6
  8.1 0.7 %copy-done.6 = f32[512]{0:T(512)S(1)} copy-done((f32[512]{0:T(512)S(1)}, f32[512]{0:T(512)}, u32[]{:S(2)}) %copy-start.6) | copy-done | bytes 2072
  8.8 0.0 copy-start.7
  8.8 0.7 %copy-done.7 = s32[4]{0:T(128)S(1)} copy-done((s32[4]{0:T(128)S(1)}, s32[4]{0:T(128)}, u32[]{:S(2)}) %copy-start.7) | copy-done | bytes 40
  9.5 36.4 %shard_map.136 = bf16[64,224]{1,0:T(8,128)(2,1)S(1)} custom-call(s32[1,512]{1,0:T(1,128)S(1)} %bitcast.4, s32[64,1]{1,0:T(8,128)S(1)} %copy.15.request_slot, bf16[4,3584]{1,0:T(4,128)(2,1)S(1)} %copy-done.2, bf16[4,3584]{1,0:T(4,128)(2,1)S(1)} %copy-done.3, s32[4]{0:T(128)S(1)} %copy-done.7, f32[1,3584]{1,0:T(1,128)S(1)} %reshape.17.norm_gain, ...), custom_call_target="tpu_custom_call" | custom-call | tf_op jit(solution)/shard_map/pallas_call | solution.py:376
  45.9 0.6 %copy.18 = bf16[64,224]{1,0:T(8,128)(2,1)} copy(bf16[64,224]{1,0:T(8,128)(2,1)S(1)} %shard_map.136) | data formatting | bytes 57344
Async XLA Ops:
  0.0 5.3 %copy-start.1 = (bf16[4,4,128,128]{3,2,1,0:T(8,128)(2,1)S(1)}, bf16[4,4,128,128]{3,2,1,0:T(8,128)(2,1)}, u32[]{:S(2)}) copy-start(bf16[4,4,128,128]{3,2,1,0:T(8,128)(2,1)} %value_cache_hbm.1) | copy-start | bytes 1572868
  0.0 5.3 %copy-start = (bf16[4,4,128,128]{3,2,1,0:T(8,128)(2,1)S(1)}, bf16[4,4,128,128]{3,2,1,0:T(8,128)(2,1)}, u32[]{:S(2)}) copy-start(bf16[4,4,128,128]{3,2,1,0:T(8,128)(2,1)} %key_cache_hbm.1) | copy-start | bytes 1572868
  5.3 0.7 %copy-start.2 = (bf16[4,3584]{1,0:T(4,128)(2,1)S(1)}, bf16[4,3584]{1,0:T(4,128)(2,1)}, u32[]{:S(2)}) copy-start(bf16[4,3584]{1,0:T(4,128)(2,1)} %new_rows.1) | copy-start | bytes 86020
  6.0 0.7 %copy-start.3 = (bf16[4,3584]{1,0:T(4,128)(2,1)S(1)}, bf16[4,3584]{1,0:T(4,128)(2,1)}, u32[]{:S(2)}) copy-start(bf16[4,3584]{1,0:T(4,128)(2,1)} %queries.1) | copy-start | bytes 86020
  6.8 0.7 %copy-start.4 = (s32[512,1]{0,1:T(1,128)S(1)}, s32[512,1]{0,1:T(1,128)}, u32[]{:S(2)}) copy-start(s32[512,1]{0,1:T(1,128)} %param.15) | copy-start | bytes 6148
  7.5 0.7 %copy-start.5 = (f32[512]{0:T(512)S(1)}, f32[512]{0:T(512)}, u32[]{:S(2)}) copy-start(f32[512]{0:T(512)} %param.25) | copy-start | bytes 6148
  8.1 0.7 %copy-start.6 = (f32[512]{0:T(512)S(1)}, f32[512]{0:T(512)}, u32[]{:S(2)}) copy-start(f32[512]{0:T(512)} %param.26) | copy-start | bytes 6148
  8.8 0.7 %copy-start.7 = (s32[4]{0:T(128)S(1)}, s32[4]{0:T(128)}, u32[]{:S(2)}) copy-start(s32[4]{0:T(128)} %cache_length.1) | copy-start | bytes 52

commit v2 on v1

--- a/solution.py
+++ b/solution.py
@@ -14,6 +14,21 @@
 
 def kernel(
     dims,
+    token_request_hbm,
+    request_slot_hbm,
+    new_rows_hbm,
+    queries_hbm,
+    cache_length_hbm,
+    norm_gain_hbm,
+    key_bias_hbm,
+    value_bias_hbm,
+    tokens_hbm,
+    key_weight_hbm,
+    value_weight_hbm,
+    out_weight_hbm,
+    key_cache_hbm,
+    value_cache_hbm,
+    out,
     token_request,
     request_slot,
     new_rows,
@@ -22,13 +37,7 @@
     norm_gain,
     key_bias,
     value_bias,
-    tokens_hbm,
-    key_weight_hbm,
-    value_weight_hbm,
-    out_weight_hbm,
-    key_cache_hbm,
-    value_cache_hbm,
-    out,
+    gain_row,
     tok,
     kw,
     vw,
@@ -88,6 +97,16 @@
         loads.append(c)
         return c
 
+    q_load = load(queries_hbm, queries)
+    request_load = load(token_request_hbm, token_request)
+    slot_load = load(request_slot_hbm, request_slot)
+    small_loads = [
+        load(norm_gain_hbm, norm_gain),
+        load(new_rows_hbm, new_rows),
+        load(cache_length_hbm, cache_length),
+        load(key_bias_hbm, key_bias),
+        load(value_bias_hbm, value_bias),
+    ]
     tok_loads = [
         load(tokens_hbm.at[pl.ds(c * chunk, chunk)], tok.at[pl.ds(c * chunk, chunk)])
         for c in range(chunks)
@@ -104,6 +123,7 @@
         pl.semaphore_signal(barrier, inc=1, device_id=peer(ahead(i)), device_id_type=MESH)
 
     qstage[...] = jnp.zeros_like(qstage)
+    q_load.wait()
     q_wide = queries[...].astype(f32)
     for g in range(kv_heads):
         for j in range(group):
@@ -114,10 +134,22 @@
     for g in range(kv_heads):
         qall[0, g] = qstage[g].astype(bf16)
 
-    slot_total = request_slot.shape[0]
+    slot_total = request_slot.shape[1]
+    request_load.wait()
+    slot_load.wait()
+    square = (slot_total, slot_total)
+    slot_column = jnp.sum(
+        jnp.where(
+            lax.broadcasted_iota(jnp.int32, square, 0) == lax.broadcasted_iota(jnp.int32, square, 1),
+            request_slot[...].astype(f32),
+            0.0,
+        ),
+        axis=1,
+        keepdims=True,
+    )
     matches = token_request[...] == lax.broadcasted_iota(jnp.int32, (slot_total, tok_dev), 0)
     slot_row = jnp.sum(
-        jnp.where(matches, request_slot[...].astype(f32), 0.0), axis=0, keepdims=True
+        jnp.where(matches, slot_column, 0.0), axis=0, keepdims=True
     ).astype(jnp.int32)
     slots[0] = jnp.broadcast_to(slot_row, (8, tok_dev))
 
@@ -136,7 +168,12 @@
         q_copies[i] = remote(qall.at[0], qall.at[i], qs_sem.at[i], qr_sem.at[i], peer(ahead(i)))
     slot_copy = remote(slots.at[0], slots.at[1], sib_s.at[2], sib_r.at[2], {"seq": sibling})
 
-    gain = norm_gain[...]
+    for c in small_loads:
+        c.wait()
+    lanes = norm_gain.shape[1]
+    for n in range(norm_gain.shape[0]):
+        gain_row[:, n * lanes : (n + 1) * lanes] = norm_gain[n : n + 1, :]
+    gain = gain_row[...]
 
     def normed(x):
         power = jnp.mean(x * x, axis=-1, keepdims=True)
@@ -238,7 +275,7 @@
     vc_load.wait()
     row_of = lax.broadcasted_iota(jnp.int32, (block, 128), 0) % rows_here
     place = lax.broadcasted_iota(jnp.int32, (block, 128), 1)
-    visible = [(row_of == r) & (place < cache_length[r]) for r in range(rows_here)]
+    visible = [(row_of == r) & (place < cache_length[0:1, r : r + 1]) for r in range(rows_here)]
     own = []
     for g in range(kv_heads):
         hf, gl = g // per_half, g % per_half
@@ -326,7 +363,9 @@
         pick = jnp.where(row_at == want, 1.0, 0.0).astype(bf16)
         a = jnp.dot(pick, flat, preferred_element_type=f32).astype(bf16)
         span = group * head_dim
-        term = jnp.dot(a, ow[g * span : (g + 1) * span, :], preferred_element_type=f32)
+        term = lax.dot_general(
+            a, ow[:, g * span : (g + 1) * span], NT, preferred_element_type=f32
+        )
         acc = term if acc is None else acc + term
     out[...] = acc.astype(bf16)
 
@@ -369,20 +408,28 @@
     block = 32
     f32, bf16, i32 = jnp.float32, jnp.bfloat16, jnp.int32
     vmem = pl.BlockSpec(memory_space=pltpu.VMEM)
-    smem = pl.BlockSpec(memory_space=pltpu.SMEM)
-    hbm = pl.BlockSpec(memory_space=pl.ANY)
+    hbm = pl.BlockSpec(memory_space=pltpu.HBM)
     dma = pltpu.SemaphoreType.DMA
     dims = (nk, rows_here, kv_heads, group, head_dim)
     return pl.pallas_call(
         functools.partial(kernel, dims),
         out_shape=jax.ShapeDtypeStruct((slot_count, out_weight.shape[1]), bf16),
-        in_specs=[vmem, vmem, vmem, vmem, smem, vmem, vmem, vmem] + [hbm] * 6,
+        in_specs=[hbm] * 14,
         out_specs=vmem,
         scratch_shapes=[
+            pltpu.VMEM((1, tok_dev), i32),
+            pltpu.VMEM((1, slot_count), i32),
+            pltpu.VMEM(new_rows.shape, bf16),
+            pltpu.VMEM(queries.shape, bf16),
+            pltpu.VMEM((1, rows_here), i32),
+            pltpu.VMEM((width // 128, 128), f32),
+            pltpu.VMEM((1, kv_width), f32),
+            pltpu.VMEM((1, kv_width), f32),
+            pltpu.VMEM((1, width), f32),
             pltpu.VMEM((tok_dev, width), bf16),
             pltpu.VMEM((width, kv_width), bf16),
             pltpu.VMEM((width, kv_width), bf16),
-            pltpu.VMEM(out_weight.shape, bf16),
+            pltpu.VMEM(out_weight.shape[::-1], bf16),
             pltpu.VMEM(key_cache.shape, bf16),
             pltpu.VMEM(value_cache.shape, bf16),
             pltpu.VMEM((tok_dev + 16, width), bf16),
@@ -397,7 +444,7 @@
             pltpu.VMEM((2, nk, 8, 128), f32),
             pltpu.VMEM((16, group * head_dim), f32),
             pltpu.VMEM((seq_count, 16, group * head_dim), bf16),
-            dma((9,)),
+            dma((17,)),
             dma((nk,)),
             dma((nk,)),
             dma((3,)),
@@ -412,21 +459,21 @@
             dma((nk,)),
         ],
         compiler_params=pltpu.CompilerParams(
-            collective_id=0, has_side_effects=True, vmem_limit_bytes=52 * 1024 * 1024
+            collective_id=0, has_side_effects=True, vmem_limit_bytes=64 * 1024 * 1024
         ),
     )(
         token_request.reshape(1, tok_dev),
-        request_slot.reshape(slot_count, 1),
+        request_slot.reshape(1, slot_count),
         new_rows,
         queries,
-        cache_length,
-        norm_gain.reshape(1, width),
+        cache_length.reshape(1, rows_here),
+        norm_gain.reshape(width // 128, 128),
         key_bias.reshape(1, kv_width),
         value_bias.reshape(1, kv_width),
         tokens,
         key_weight,
         value_weight,
-        out_weight,
+        out_weight.T,
         key_cache,
         value_cache,
     )

time: 46.9 us -> 38.2 us (0.81)
  local copies, waits for them, and re-layouts: 10.1 us -> 1.38 us
    unnamed x18 -> x1, local copies, waits for them, and re-layouts: 8.52 us -> 1.38 us
    reshape x2 -> x0, local copies, waits for them, and re-layouts: 1.56 us -> none  [the longest x1 0.82 us: body(): norm_gain.reshape(1, width)]
where the time goes in v2:
time: 38.2 us; the launch traced here: 38 us
  Pallas kernels  36.6 us (96%)
  local copies, waits for them, and re-layouts  1.38 us (4%)
    pallas_call x1, Pallas kernels, body(): pl.pallas_call(functools.partial(kernel, dims), out_shape=jax.ShapeDtypeS...  36.6 us
    unnamed x1, local copies, waits for them, and re-layouts  1.38 us

profile of v2, /device:TPU:1, one launch (start us, length us, event | category | flops | bytes accessed | tf_op | source)
XLA Modules:
  0.0 38.0 jit_solution(4756678047745759028)
XLA Ops:
  0.0 36.6 %shard_map.136 = bf16[64,224]{1,0:T(8,128)(2,1)} custom-call(s32[1,512]{1,0:T(1,128)} %bitcast.9, s32[1,64]{1,0:T(1,128)} %bitcast.12, bf16[4,3584]{1,0:T(4,128)(2,1)} %new_rows_hbm.1, bf16[4,3584]{1,0:T(4,128)(2,1)} %queries_hbm.1, s32[1,4]{1,0:T(1,128)} %bitcast.13, f32[28,128]{1,0:T(8,128)} %bitcast.8, f32[1,512]{1,0:T(1,128)} %bitcast.10, ...), custom_call_target="tpu_custom_call" | custom-call | tf_op jit(solution)/shard_map/pallas_call | solution.py:414
  36.6 1.4 %copy.16 = bf16[64,224]{1,0:T(8,128)(2,1)} copy(bf16[64,224]{1,0:T(8,128)(2,1)} %shard_map.136) | data formatting | bytes 57344

commit v3 on v2

--- a/solution.py
+++ b/solution.py
@@ -52,8 +52,6 @@
     kvr,
     part,
     rpart,
-    stat,
-    rstat,
     hstage,
     hall,
     load_sem,
@@ -63,8 +61,6 @@
     sib_r,
     ps_sem,
     pr_sem,
-    ss_sem,
-    sr_sem,
     hs_sem,
     hr_sem,
     fs_sem,
@@ -185,22 +181,34 @@
     xn[tok_dev : tok_dev + 16, :] = normed(fresh)
     for c in range(chunks):
         tok_loads[c].wait()
-
-        @pl.loop(c * chunk // 16, (c + 1) * chunk // 16)
-        def _(b):
-            at = pl.ds(pl.multiple_of(b * 16, 16), 16)
-            xn[at, :] = normed(tok[at, :].astype(f32))
-
+        if c < chunks // 2:
+
+            @pl.loop(c * chunk // 16, (c + 1) * chunk // 16, unroll=2)
+            def _(b):
+                at = pl.ds(pl.multiple_of(b * 16, 16), 16)
+                xn[at, :] = normed(tok[at, :].astype(f32))
+
+    kw_load.wait()
+    vw_load.wait()
+    half = kw.shape[1] // 2
+    middle = tok_dev // 2
+
+    def project(hf, n, low, high):
+        cols = slice(hf * half, (hf + 1) * half)
+        w, b = ((kw, key_bias), (vw, value_bias))[n]
+        kvl[hf, low:high, n * half : (n + 1) * half] = (
+            jnp.dot(xn[low:high, :], w[:, cols], preferred_element_type=f32) + b[:, cols]
+        ).astype(bf16)
+
+    left = list(range(middle, tok_dev, 16))
+    for n in range(4):
+        for at in left[n * len(left) // 4 : (n + 1) * len(left) // 4]:
+            xn[at : at + 16, :] = normed(tok[at : at + 16, :].astype(f32))
+        project(n // 2, n % 2, 0, middle)
     kv_copies = []
-    half = kw.shape[1] // 2
     for hf in range(2):
-        cols = slice(hf * half, (hf + 1) * half)
-        for n, (w, b, w_load) in enumerate(((kw, key_bias, kw_load), (vw, value_bias, vw_load))):
-            if hf == 0:
-                w_load.wait()
-            kvl[hf, :, n * half : (n + 1) * half] = (
-                jnp.dot(xn[...], w[:, cols], preferred_element_type=f32) + b[:, cols]
-            ).astype(bf16)
+        for n in range(2):
+            project(hf, n, middle, tok_dev + 16)
         kv_copies.append(
             remote(
                 kvl.at[hf, pl.ds(0, tok_dev)],
@@ -220,6 +228,7 @@
     per_chunk = min(4, nk)
     chunk_rows = per_chunk * block
     p_copies = {}
+    lse_of = [{} for _ in range(nk // per_chunk)]
     for hf in range(2):
         kv_copies[hf].wait_recv()
         for q0 in range(0, nk, per_chunk):
@@ -247,29 +256,28 @@
                     p_l.astype(bf16), kvl[hf, :tok_dev, vcols], preferred_element_type=f32
                 ) + jnp.dot(p_r.astype(bf16), kvr[hf, :, vcols], preferred_element_type=f32)
                 o = (o / total).astype(bf16)
-                part[hf, q0 : q0 + per_chunk, gl] = o.reshape(per_chunk, block, head_dim)
+                part[q0 : q0 + per_chunk, g] = o.reshape(per_chunk, block, head_dim)
                 lses.append(top + jnp.log(total))
-            which = lax.broadcasted_iota(jnp.int32, (chunk_rows, 128), 1)
-            packed = jnp.where(which == 0, lses[0], jnp.where(which == 1, lses[1], 0.0))
-            stat[hf, q0 // per_chunk] = packed.T[:8, :]
-            for i in range(q0, q0 + per_chunk):
-                if i > 0:
-                    p_copies[hf, i] = (
-                        remote(
-                            part.at[hf, i],
-                            rpart.at[hf, i],
-                            ps_sem.at[hf, i],
-                            pr_sem.at[hf, i],
-                            peer(behind(i)),
-                        ),
-                        remote(
-                            stat.at[hf, i // per_chunk],
-                            rstat.at[hf, i],
-                            ss_sem.at[hf, i],
-                            sr_sem.at[hf, i],
-                            peer(behind(i)),
-                        ),
-                    )
+            for gl in range(per_half):
+                lse_of[q0 // per_chunk][hf * per_half + gl] = lses[gl]
+    for c in range(nk // per_chunk):
+        which = lax.broadcasted_iota(jnp.int32, (chunk_rows, 128), 1)
+        packed = jnp.zeros((chunk_rows, 128), f32)
+        for g in range(kv_heads):
+            packed = jnp.where(which == g, lse_of[c][g], packed)
+        rest = packed.T[:8, :]
+        terms = []
+        for _ in range(3):
+            term = rest.astype(bf16).astype(f32)
+            terms.append(term)
+            rest = rest - term
+        coded = jnp.concatenate(terms + [jnp.zeros((block - 24, 128), f32)], axis=0).astype(bf16)
+        for i in range(c * per_chunk, (c + 1) * per_chunk):
+            part[i, kv_heads] = coded
+            if i > 0:
+                p_copies[i] = remote(
+                    part.at[i], rpart.at[i], ps_sem.at[i], pr_sem.at[i], peer(behind(i))
+                )
 
     kc_load.wait()
     vc_load.wait()
@@ -301,23 +309,25 @@
             )
         own.append((top, total, acc))
 
+    for i in range(1, nk):
+        p_copies[i].wait_recv()
+    stats = []
+    for i in range(nk):
+        coded = (rpart[i, kv_heads] if i > 0 else part[0, kv_heads]).astype(f32)
+        stats.append(coded[0:8] + coded[8:16] + coded[16:24])
+    flat = jnp.concatenate(stats, axis=0)
+    pad = -(nk * 8) % 128
+    if pad:
+        flat = jnp.concatenate([flat, jnp.zeros((pad, 128), f32)], axis=0)
+    turned = flat.T
     for hf in range(2):
-        for i in range(1, nk):
-            for c in p_copies[hf, i]:
-                c.wait_recv()
-        rstat[hf, 0] = stat[hf, 0]
-        flat = rstat[hf].reshape(nk * 8, 128)
-        pad = -(nk * 8) % 128
-        if pad:
-            flat = jnp.concatenate([flat, jnp.zeros((pad, 128), f32)], axis=0)
-        turned = flat.T
         for gl in range(per_half):
             g = hf * per_half + gl
             top, total, acc = own[g]
             cols = []
             for i in range(nk):
                 r0 = (i % per_chunk) * block
-                cols.append(turned[r0 : r0 + block, i * 8 + gl : i * 8 + gl + 1])
+                cols.append(turned[r0 : r0 + block, i * 8 + g : i * 8 + g + 1])
             best = top
             for col in cols:
                 best = jnp.maximum(best, col)
@@ -327,7 +337,7 @@
             for i in range(nk):
                 w = jnp.exp(cols[i] - best)
                 total = total + w
-                piece = part[hf, 0, gl] if i == 0 else rpart[hf, i, gl]
+                piece = part[0, g] if i == 0 else rpart[i, g]
                 acc = acc + w * piece.astype(f32)
             result = acc / total
             for j in range(group):
@@ -372,9 +382,7 @@
     for i in range(1, nk):
         q_copies[i].wait_send()
         h_copies[i].wait_send()
-        for hf in range(2):
-            for c in p_copies[hf, i]:
-                c.wait_send()
+        p_copies[i].wait_send()
     for i in range(nk):
         f_copies[i].wait_send()
     slot_copy.wait_send()
@@ -438,10 +446,8 @@
             pltpu.VMEM((2, 8, tok_dev), i32),
             pltpu.VMEM((2, tok_dev + 16, kv_width), bf16),
             pltpu.VMEM((2, tok_dev, kv_width), bf16),
-            pltpu.VMEM((2, nk, kv_heads // 2, block, head_dim), bf16),
-            pltpu.VMEM((2, nk, kv_heads // 2, block, head_dim), bf16),
-            pltpu.VMEM((2, nk // 4, 8, 128), f32),
-            pltpu.VMEM((2, nk, 8, 128), f32),
+            pltpu.VMEM((nk, kv_heads + 1, block, head_dim), bf16),
+            pltpu.VMEM((nk, kv_heads + 1, block, head_dim), bf16),
             pltpu.VMEM((16, group * head_dim), f32),
             pltpu.VMEM((seq_count, 16, group * head_dim), bf16),
             dma((17,)),
@@ -449,10 +455,8 @@
             dma((nk,)),
             dma((3,)),
             dma((3,)),
-            dma((2, nk)),
-            dma((2, nk)),
-            dma((2, nk)),
-            dma((2, nk)),
+            dma((nk,)),
+            dma((nk,)),
             dma((nk,)),
             dma((nk,)),
             dma((nk,)),

time: 38.2 us -> 36.6 us (0.958)
  Pallas kernels: 36.6 us -> 35 us
    pallas_call x1, Pallas kernels: 36.6 us -> 35 us  [body(): pl.pallas_call(functools.partial(kernel, dims), out_shape=jax.ShapeDtypeS...]
where the time goes in v3:
time: 36.6 us; the launch traced here: 36.4 us
  Pallas kernels  35 us (96%)
  local copies, waits for them, and re-layouts  1.38 us (4%)
    pallas_call x1, Pallas kernels, body(): pl.pallas_call(functools.partial(kernel, dims), out_shape=jax.ShapeDtypeS...  35 us
    unnamed x1, local copies, waits for them, and re-layouts  1.38 us

profile of v3, /device:TPU:1, one launch (start us, length us, event | category | flops | bytes accessed | tf_op | source)
XLA Modules:
  0.0 36.4 jit_solution(5312133220783090161)
XLA Ops:
  0.0 35.0 %shard_map.136 = bf16[64,224]{1,0:T(8,128)(2,1)} custom-call(s32[1,512]{1,0:T(1,128)} %bitcast.9, s32[1,64]{1,0:T(1,128)} %bitcast.12, bf16[4,3584]{1,0:T(4,128)(2,1)} %new_rows_hbm.1, bf16[4,3584]{1,0:T(4,128)(2,1)} %queries_hbm.1, s32[1,4]{1,0:T(1,128)} %bitcast.13, f32[28,128]{1,0:T(8,128)} %bitcast.8, f32[1,512]{1,0:T(1,128)} %bitcast.10, ...), custom_call_target="tpu_custom_call" | custom-call | tf_op jit(solution)/shard_map/pallas_call | solution.py:422
  35.0 1.4 %copy.16 = bf16[64,224]{1,0:T(8,128)(2,1)} copy(bf16[64,224]{1,0:T(8,128)(2,1)} %shard_map.136) | data formatting | bytes 57344
